TPU v7x, 512 devices: a whole 4x4x16 slice. The times are simulated.
512 devices in a mesh: scene: 64 (over z_lo, x, core), tile: 8 (over z_hi, y).
Axes of the slice: x: 4, y: 4, z: 16 (z_hi: 2, z_lo: 8; z = z_hi * 8 + z_lo), core: 2. Of those that a mesh axis runs over, the one named last changes fastest.
Arguments:
- radiance: bfloat16 [512, 8, 10, 8192], P(('scene', 'tile')), may hold values from -8 to 8
- cloud_weight: int32 [512, 8, 8192], P(('scene', 'tile')), may hold values from 0 to 15
- footprint: int32 [512, 8], replicated, may hold values from 0 to 63, as said below
Outputs:
- composite: bfloat16 [64, 10, 8192], P('tile', None, 'scene')
- overview_one: bfloat16 [64, 10, 64, 32], P('tile')
- overview_two: bfloat16 [64, 10, 32, 16], P('tile')
- overview_three: bfloat16 [64, 10, 16, 8], P('tile')
- overview_four: bfloat16 [64, 10, 8, 4], P('tile')
- overview_five: bfloat16 [64, 10, 4, 2], P('tile')
Inputs may be any that keep to these rules, and one draw needn't show every extreme that they name: `footprint`: each row names 8 different tiles; at most 2 tiles of a row share the value of tile // 8, and in every row some such group holds exactly 2 tiles.
All inputs are finite; a program needn't handle non-finite values.
Results may differ from a plain program's by a relative error of at most 0.012.
Values may be sent and summed in bfloat16 or wider, within the bound.
A program may use at most 128 MiB of HBM per device.

v0:
```python
import jax
import jax.numpy as jnp
from jax import lax
from jax.sharding import PartitionSpec as P

K = 8
TILE_DEV = 8
COLS = 64


def average_pool(values):
    height = values.shape[-2]
    width = values.shape[-1]
    shaped = values.astype(jnp.float32).reshape(values.shape[:-2] + (height // 2, 2, width // 2, 2))
    return jnp.mean(shaped, axis=(-3, -1)).astype(jnp.bfloat16)


def owner_rank(tile_rows, tile_dev):
    owner_of = tile_rows // tile_dev
    same_owner = owner_of[..., :, None] == owner_of[..., None, :]
    positions = jnp.arange(tile_rows.shape[-1])
    earlier = positions[None, :] < positions[:, None]
    rank_of = jnp.sum(jnp.logical_and(same_owner, earlier), axis=-1)
    return (owner_of, rank_of)


def slot_table(tile_rows, owner_index, capacity, tile_dev):
    owner_of, rank_of = owner_rank(tile_rows, tile_dev)
    matched = owner_of == owner_index
    local_tile = tile_rows - owner_index * tile_dev
    by_rank = jnp.logical_and(
        matched[..., None], rank_of[..., None] == jnp.arange(capacity)
    ).astype(jnp.float32)
    by_tile = (local_tile[..., None] == jnp.arange(tile_dev)).astype(jnp.float32)
    return jnp.einsum("skc,sku->scu", by_rank, by_tile, precision=lax.Precision.HIGHEST)


def on_device(radiance, cloud_weight, footprint):
    owners = lax.axis_size("tile")
    capacity = max(2, 2 * K // owners)
    scene_index = lax.axis_index("scene")
    tile_index = lax.axis_index("tile")
    device = scene_index * owners + tile_index
    pixels = radiance.shape[3]
    bands = radiance.shape[2]
    my_row = lax.dynamic_slice_in_dim(footprint, device, 1, 0)[0]
    owner_of, rank_of = owner_rank(my_row, TILE_DEV)
    slot_of = owner_of * capacity + rank_of
    placement = (jnp.arange(owners * capacity)[:, None] == slot_of[None, :]).astype(jnp.bfloat16)
    send_rad = jnp.einsum("pk,kbq->pbq", placement, radiance[0], preferred_element_type=jnp.float32)
    send_rad = send_rad.astype(jnp.bfloat16).reshape(owners, capacity, bands, pixels)
    weight_bf = cloud_weight[0].astype(jnp.bfloat16)
    send_weight = jnp.dot(placement, weight_bf, preferred_element_type=jnp.float32)
    send_weight = send_weight.astype(jnp.bfloat16).reshape(owners, capacity, 1, pixels)
    got_rad, got_weight = (
        lax.all_to_all(send_rad, "tile", split_axis=0, concat_axis=0, tiled=True),
        lax.all_to_all(send_weight, "tile", split_axis=0, concat_axis=0, tiled=True),
    )
    source_rows = lax.dynamic_slice_in_dim(footprint, scene_index * owners, owners, 0)
    assign = slot_table(source_rows, tile_index, capacity, TILE_DEV)
    weight_float = got_weight[:, :, 0, :].astype(jnp.float32)
    product = weight_float[:, :, None, :] * got_rad.astype(jnp.float32)
    local_sums = jnp.einsum("scu,scbq->ubq", assign, product, precision=lax.Precision.HIGHEST)
    local_totals = jnp.einsum("scu,scq->uq", assign, weight_float, precision=lax.Precision.HIGHEST)
    weighted_sums, weight_totals = (
        lax.psum_scatter(local_sums, "scene", scatter_dimension=2, tiled=True),
        lax.psum_scatter(local_totals, "scene", scatter_dimension=1, tiled=True),
    )
    composite = (weighted_sums / jnp.maximum(weight_totals, 1.0)[:, None, :]).astype(jnp.bfloat16)
    local_rows = composite.shape[2] // COLS
    grid = composite.reshape(composite.shape[0], bands, local_rows, COLS)
    whole_grid = lax.all_gather(grid, "scene", axis=2, tiled=True)
    overview_one = average_pool(whole_grid)
    overview_two = average_pool(overview_one)
    overview_three = average_pool(overview_two)
    overview_four = average_pool(overview_three)
    overview_five = average_pool(overview_four)
    return (composite, overview_one, overview_two, overview_three, overview_four, overview_five)


def solution(mesh):
    in_specs = (P(("scene", "tile"), None, None, None), P(("scene", "tile"), None, None), P())
    out_specs = (
        P("tile", None, "scene"),
        P("tile", None, None, None),
        P("tile", None, None, None),
        P("tile", None, None, None),
        P("tile", None, None, None),
        P("tile", None, None, None),
    )
    return jax.shard_map(
        on_device, mesh=mesh, in_specs=in_specs, out_specs=out_specs, check_vma=False
    )
```

profile of v0, /device:TPU:1, one launch (start us, length us, event | category | flops | bytes accessed | tf_op | source)
XLA Modules:
  0.0 1196.3 jit_solution(4927155921936412516)
XLA Ops:
  7.2 0.9 constant_dynamic-slice_fusion
  8.1 0.1 copy.108
  8.2 0.2 convert_reduce_fusion.5
  8.4 1.3 convolution_convert_fusion.1
  9.7 0.9 reshape.103
  10.5 18.3 %all-to-all-start = ((bf16[8,2,1,8192]{3,1,2,0:T(2,128)(2,1)}), bf16[8,2,1,8192]{3,1,2,0:T(2,128)(2,1)S(1)}, u32[]{:S(2)}, u32[]{:S(2)}) async-start(bf16[8,2,1,8192]{3,1,2,0:T(2,128)(2,1)} %bitcast.6), calls=%async_computation | async-start | bytes 524288 | tf_op jit(solution)/shard_map/all_to_all | solution.py:57
  28.8 2.4 convolution_convert_fusion
  31.2 5.4 reshape.104
  36.5 7.5 copy.94
  44.0 0.1 all-to-all-done
  44.1 13.9 %all-to-all-start.1 = ((bf16[8,2,10,8192]{3,1,2,0:T(2,128)(2,1)}), bf16[8,2,10,8192]{3,1,2,0:T(2,128)(2,1)}, u32[]{:S(2)}, u32[]{:S(2)}) async-start(bf16[8,2,10,8192]{3,1,2,0:T(2,128)(2,1)} %copy.94), calls=%async_computation.1 | async-start | bytes 5242880 | tf_op jit(solution)/shard_map/all_to_all | solution.py:56
  58.0 0.0 reduce-scatter.5.cloned.1.call-start
  58.0 0.1 dynamic-slice_subtract_fusion
  58.1 0.1 copy.90
  58.2 0.1 broadcast_compare_fusion
  58.3 0.1 copy.87
  58.4 0.1 copy.88
  58.4 0.3 convert_reduce_fusion.4
  58.7 0.2 fusion.9
  58.9 0.1 copy.96
  59.0 1.1 convolution_bitcast_fusion.1
  60.1 0.0 reduce-scatter.3.cloned.1.call-start
  60.1 0.2 bitcast_convert_fusion
  60.3 47.7 %all-to-all-done.1 = bf16[8,2,10,8192]{3,1,2,0:T(2,128)(2,1)} async-done(((bf16[8,2,10,8192]{3,1,2,0:T(2,128)(2,1)}), bf16[8,2,10,8192]{3,1,2,0:T(2,128)(2,1)}, u32[]{:S(2)}, u32[]{:S(2)}) %all-to-all-start.1) | async-done | bytes 2621472 | tf_op jit(solution)/shard_map/all_to_all | solution.py:56
  108.0 7.3 convolution_bitcast_fusion
  115.3 0.0 reduce-scatter.3.cloned.1.call-update
  115.3 0.2 all-gather.2.cloned.1.call-start
  115.5 429.0 %reduce-scatter.5.cloned.1.call-done = f32[8,128]{1,0:T(8,128)} async-done(((f32[8,8192]{1,0:T(8,128)}), f32[8,128]{1,0:T(8,128)}) %reduce-scatter.5.cloned.1.call-update) | async-done | bytes 4112 | tf_op jit(solution)/shard_map/reduce_scatter | solution.py:67
  544.5 0.7 broadcast_maximum_fusion
  545.2 449.9 %reduce-scatter.3.cloned.1.call-done = f32[8,10,128]{2,0,1:T(8,128)} async-done(((f32[8,10,8192]{2,0,1:T(8,128)}), f32[8,10,128]{2,0,1:T(8,128)}) %reduce-scatter.3.cloned.1.call-update) | async-done | bytes 40976 | tf_op jit(solution)/shard_map/reduce_scatter | solution.py:66
  995.1 0.8 divide_convert_fusion
  995.9 0.1 reshape.105
  996.0 0.6 copy.99
  996.6 125.3 %all-gather.2.cloned.1.call-done = bf16[8,10,128,64]{3,0,1,2:T(8,128)(2,1)} async-done(((bf16[8,10,2,64]{3,0,1,2:T(8,128)(2,1)}), bf16[8,10,128,64]{3,0,1,2:T(8,128)(2,1)}) %all-gather.2.cloned.1.call-update) | async-done | bytes 1310736 | tf_op jit(solution)/shard_map/all_gather | solution.py:72
  1121.9 4.4 copy.100
  1126.3 25.0 %copy.101 = f32[8,10,128,64]{1,0,3,2:T(8,128)} copy(bf16[8,10,128,64]{2,3,1,0:T(8,128)(2,1)S(1)} %copy.100) | data formatting | bytes 3932160 | tf_op jit(solution)/shard_map/reshape | solution.py:14
  1151.3 16.3 %reduce_sum.68 = f32[8,10,64,32]{1,0,3,2:T(8,128)} reduce(f32[8,10,64,2,32,2]{1,0,5,4,3,2:T(8,128)} %bitcast.56, f32[]{:T(128)} %constant.53.clone.1), dimensions={3,5}, to_apply=%region_4.5 | reduce | flops 491520 | bytes 3276804 | tf_op jit(solution)/shard_map/reduce_sum | solution.py:15
  1167.6 6.4 multiply_convert_fusion
  1174.0 7.0 copy.102
  1181.0 3.4 convert_reduce_fusion
  1184.4 0.2 multiply_convert_fusion.1
  1184.6 2.3 copy.103
  1186.9 0.2 convert_reduce_fusion.1
  1187.1 0.1 multiply_convert_fusion.2
  1187.2 1.2 copy.104
  1188.4 0.1 convert_reduce_fusion.2
  1188.5 0.7 copy.105
  1189.2 0.6 copy.106
  (17 shorter events, 0.1 us)
Async XLA Ops:
  7.2 21.7 %copy-start = (bf16[1,8,10,8192]{3,1,2,0:T(8,128)(2,1)S(1)}, bf16[1,8,10,8192]{3,1,2,0:T(8,128)(2,1)}, u32[]{:S(2)}) copy-start(bf16[1,8,10,8192]{3,1,2,0:T(8,128)(2,1)} %param.3) | copy-start | bytes 3932164
  10.5 33.5 %all-to-all-start = ((bf16[8,2,1,8192]{3,1,2,0:T(2,128)(2,1)}), bf16[8,2,1,8192]{3,1,2,0:T(2,128)(2,1)S(1)}, u32[]{:S(2)}, u32[]{:S(2)}) async-start(bf16[8,2,1,8192]{3,1,2,0:T(2,128)(2,1)} %bitcast.6), calls=%async_computation | async-start | bytes 524288 | tf_op jit(solution)/shard_map/all_to_all | solution.py:57
  44.0 14.0 %copy-start.3 = (s32[512,8]{0,1:T(8,128)S(1)}, s32[512,8]{0,1:T(8,128)}, u32[]{:S(2)}) copy-start(s32[512,8]{0,1:T(8,128)} %param.5) | copy-start | bytes 49156
  44.1 63.9 %all-to-all-start.1 = ((bf16[8,2,10,8192]{3,1,2,0:T(2,128)(2,1)}), bf16[8,2,10,8192]{3,1,2,0:T(2,128)(2,1)}, u32[]{:S(2)}, u32[]{:S(2)}) async-start(bf16[8,2,10,8192]{3,1,2,0:T(2,128)(2,1)} %copy.94), calls=%async_computation.1 | async-start | bytes 5242880 | tf_op jit(solution)/shard_map/all_to_all | solution.py:56
  58.0 486.6 %reduce-scatter.5.cloned.1.call-start = ((), (), s32[]{:S(2)}) async-start(), calls=%async_computation.5 | async-start | bytes 266240 | tf_op jit(solution)/shard_map/reduce_scatter | solution.py:67
  60.1 935.0 %reduce-scatter.3.cloned.1.call-start = ((), (), s32[]{:S(2)}) async-start(), calls=%async_computation.4 | async-start | bytes 2662400 | tf_op jit(solution)/shard_map/reduce_scatter | solution.py:66
  115.3 1006.6 %all-gather.2.cloned.1.call-start = ((), (), s32[]{:S(2)}) async-start(), calls=%async_computation.6 | async-start | bytes 2662400 | tf_op jit(solution)/shard_map/all_gather | solution.py:72
  995.9 155.4 %copy-start.2 = (bf16[8,10,128]{2,0,1:T(8,128)(2,1)}, bf16[8,10,128]{2,0,1:T(8,128)(2,1)S(1)}, u32[]{:S(2)}) copy-start(bf16[8,10,128]{2,0,1:T(8,128)(2,1)S(1)} %divide_convert_fusion) | copy-start | bytes 61444
  1184.4 5.4 copy-start.1
Sparse Core Ops, SparseCore 0:
  62.2 482.3 reduce-scatter.4
  547.5 447.5 reduce-scatter.2
  997.8 124.0 all-gather.1
where the time goes:
time: 1200 us
  waiting for transfers between devices  1050 us (88%)
  local copies, waits for them, and re-layouts  56.9 us (5%)
  starting transfers between devices  32.4 us (3%)
  other arithmetic  28.9 us (2%)
  between operations  13.9 us (1%)
  matrix products  12.2 us (1%)
    reduce_scatter x1, waiting for transfers between devices, on_device(): lax.psum_scatter(local_sums, 'scene', scatter_dimension=2, tiled=True)  450 us
    reduce_scatter x1, waiting for transfers between devices, on_device(): lax.psum_scatter(local_totals, 'scene', scatter_dimension=1, tiled=True)  429 us
    all_gather x1, waiting for transfers between devices, on_device(): whole_grid = lax.all_gather(grid, 'scene', axis=2, tiled=True)  125 us
    all_to_all x1, waiting for transfers between devices, on_device(): lax.all_to_all(send_rad, 'tile', split_axis=0, concat_axis=0, tiled=True)  47.7 us
    reshape x1, local copies, waits for them, and re-layouts, average_pool(): values.astype(jnp.float32)  25 us
  transfers between devices with their start and end apart: 5, of which 5 were waited for; matrix products, arithmetic and copies ran while one was open for 2% of the time, Pallas kernels for 0%

commit v1 on v0

--- a/solution.py
+++ b/solution.py
@@ -69,7 +69,9 @@
     composite = (weighted_sums / jnp.maximum(weight_totals, 1.0)[:, None, :]).astype(jnp.bfloat16)
     local_rows = composite.shape[2] // COLS
     grid = composite.reshape(composite.shape[0], bands, local_rows, COLS)
-    whole_grid = lax.all_gather(grid, "scene", axis=2, tiled=True)
+    whole_grid = jnp.concatenate(
+        lax.all_to_all(jnp.stack([grid] * lax.axis_size("scene")), "scene", 0, 0), axis=2
+    )
     overview_one = average_pool(whole_grid)
     overview_two = average_pool(overview_one)
     overview_three = average_pool(overview_two)

time: 1200 us -> 1120 us (0.933)
  waiting for transfers between devices: 1050 us -> 926 us
  blocking collectives: 0 us -> 76.8 us
  local copies, waits for them, and re-layouts: 56.9 us -> 42.9 us
    all_gather x1 -> x0, waiting for transfers between devices: 125 us -> none  [on_device(): whole_grid = lax.all_gather(grid, 'scene', axis=2, tiled=True)]
    all_to_all x0 -> x1, blocking collectives: none -> 76.8 us  [on_device(): lax.all_to_all(jnp.stack([grid] * lax.axis_size('scene')), 'scene', 0, 0)]
    reshape x3 -> x0, local copies, waits for them, and re-layouts: 25.7 us -> none  [the longest x1 25 us: average_pool(): values.astype(jnp.float32)]
  transfers between devices with their start and end apart: 5 -> 4, of which waited for: 5 -> 4; matrix products, arithmetic and copies ran while one was open for 2% -> 2% of each run, Pallas kernels for 0% -> 0%
where the time goes in v1:
time: 1120 us
  waiting for transfers between devices  926 us (83%)
  blocking collectives  76.8 us (7%)
  local copies, waits for them, and re-layouts  42.9 us (4%)
  starting transfers between devices  32.2 us (3%)
  other arithmetic  17 us (2%)
  between operations  14.2 us (1%)
  matrix products  12.2 us (1%)
    reduce_scatter x1, waiting for transfers between devices, on_device(): lax.psum_scatter(local_sums, 'scene', scatter_dimension=2, tiled=True)  449 us
    reduce_scatter x1, waiting for transfers between devices, on_device(): lax.psum_scatter(local_totals, 'scene', scatter_dimension=1, tiled=True)  429 us
    all_to_all x1, blocking collectives, on_device(): lax.all_to_all(jnp.stack([grid] * lax.axis_size('scene')), 'scene', 0, 0)  76.8 us
    all_to_all x1, waiting for transfers between devices, on_device(): lax.all_to_all(send_rad, 'tile', split_axis=0, concat_axis=0, tiled=True)  47.4 us
  transfers between devices with their start and end apart: 4, of which 4 were waited for; matrix products, arithmetic and copies ran while one was open for 2% of the time, Pallas kernels for 0%

profile of v1, /device:TPU:1, one launch (start us, length us, event | category | flops | bytes accessed | tf_op | source)
XLA Modules:
  0.0 1121.8 jit_solution(1250129875943386022)
XLA Ops:
  7.2 0.9 constant_dynamic-slice_fusion
  8.1 0.1 copy.110
  8.2 0.2 convert_reduce_fusion.5
  8.4 1.3 convolution_convert_fusion.1
  9.6 0.9 reshape.101
  10.5 18.3 %all-to-all-start = ((bf16[8,2,1,8192]{3,1,2,0:T(2,128)(2,1)}), bf16[8,2,1,8192]{3,1,2,0:T(2,128)(2,1)S(1)}, u32[]{:S(2)}, u32[]{:S(2)}) async-start(bf16[8,2,1,8192]{3,1,2,0:T(2,128)(2,1)} %bitcast.6), calls=%async_computation | async-start | bytes 524288 | tf_op jit(solution)/shard_map/all_to_all | solution.py:57
  28.8 2.4 convolution_convert_fusion
  31.2 5.4 reshape.102
  36.5 7.5 copy.96
  44.0 0.1 all-to-all-done
  44.1 13.9 %all-to-all-start.1 = ((bf16[8,2,10,8192]{3,1,2,0:T(2,128)(2,1)}), bf16[8,2,10,8192]{3,1,2,0:T(2,128)(2,1)}, u32[]{:S(2)}, u32[]{:S(2)}) async-start(bf16[8,2,10,8192]{3,1,2,0:T(2,128)(2,1)} %copy.96), calls=%async_computation.1 | async-start | bytes 5242880 | tf_op jit(solution)/shard_map/all_to_all | solution.py:56
  58.0 0.1 dynamic-slice_subtract_fusion
  58.1 0.1 copy.92
  58.2 0.1 broadcast_compare_fusion
  58.3 0.1 copy.89
  58.4 0.1 copy.90
  58.4 0.3 convert_reduce_fusion.4
  58.7 0.2 fusion.9
  58.9 0.1 copy.98
  59.0 1.1 convolution_bitcast_fusion.1
  60.1 0.0 reduce-scatter.3.cloned.1.call-start
  60.1 0.2 bitcast_convert_fusion
  60.3 47.4 %all-to-all-done.1 = bf16[8,2,10,8192]{3,1,2,0:T(2,128)(2,1)} async-done(((bf16[8,2,10,8192]{3,1,2,0:T(2,128)(2,1)}), bf16[8,2,10,8192]{3,1,2,0:T(2,128)(2,1)}, u32[]{:S(2)}, u32[]{:S(2)}) %all-to-all-start.1) | async-done | bytes 2621472 | tf_op jit(solution)/shard_map/all_to_all | solution.py:56
  107.7 7.3 convolution_bitcast_fusion
  115.1 429.5 %reduce-scatter.5.cloned.1.call-done = f32[8,128]{1,0:T(8,128)} async-done(((f32[8,8192]{1,0:T(8,128)}), f32[8,128]{1,0:T(8,128)}) %reduce-scatter.5.cloned.1.call-update) | async-done | bytes 4112 | tf_op jit(solution)/shard_map/reduce_scatter | solution.py:67
  544.5 0.7 broadcast_maximum_fusion
  545.2 449.4 %reduce-scatter.3.cloned.1.call-done = f32[8,10,128]{2,0,1:T(8,128)} async-done(((f32[8,10,8192]{2,0,1:T(8,128)}), f32[8,10,128]{2,0,1:T(8,128)}) %reduce-scatter.3.cloned.1.call-update) | async-done | bytes 40976 | tf_op jit(solution)/shard_map/reduce_scatter | solution.py:66
  994.6 0.8 divide_convert_fusion
  995.4 0.1 stack_reshape.2
  995.5 1.8 broadcast_bitcast_fusion
  997.4 4.4 reshape.111
  1001.8 76.8 %all_to_all.15 = bf16[64,2,5120]{2,1,0:T(2,128)(2,1)} all-to-all(bf16[64,2,5120]{2,1,0:T(2,128)(2,1)S(1)} %reshape.111), channel_id=1, replica_groups=mesh['scene'=64,'tile'=8] {'scene'}, dimensions={0} | all-to-all | bytes 2621440 | tf_op jit(solution)/shard_map/all_to_all | solution.py:73
  1078.6 5.3 reshape.112
  1083.9 4.3 convert_reduce_fusion
  1088.3 3.3 copy.102
  1091.6 2.2 reduce_sum.80
  1093.8 0.1 multiply_convert_fusion.1
  1093.9 1.0 copy.104
  1094.9 7.2 copy.103
  1102.1 5.9 reduce_sum.81
  1108.0 1.8 multiply_convert_fusion
  1109.9 2.3 copy.105
  1112.1 0.2 convert_reduce_fusion.1
  1112.3 0.1 multiply_convert_fusion.2
  1112.4 1.2 copy.106
  1113.6 0.1 convert_reduce_fusion.2
  1113.7 0.7 copy.107
  1114.4 0.6 copy.108
  (17 shorter events, 0.2 us)
Async XLA Ops:
  7.2 21.7 %copy-start = (bf16[1,8,10,8192]{3,1,2,0:T(8,128)(2,1)S(1)}, bf16[1,8,10,8192]{3,1,2,0:T(8,128)(2,1)}, u32[]{:S(2)}) copy-start(bf16[1,8,10,8192]{3,1,2,0:T(8,128)(2,1)} %param.3) | copy-start | bytes 3932164
  10.5 33.6 %all-to-all-start = ((bf16[8,2,1,8192]{3,1,2,0:T(2,128)(2,1)}), bf16[8,2,1,8192]{3,1,2,0:T(2,128)(2,1)S(1)}, u32[]{:S(2)}, u32[]{:S(2)}) async-start(bf16[8,2,1,8192]{3,1,2,0:T(2,128)(2,1)} %bitcast.6), calls=%async_computation | async-start | bytes 524288 | tf_op jit(solution)/shard_map/all_to_all | solution.py:57
  44.0 14.0 %copy-start.2 = (s32[512,8]{0,1:T(8,128)S(1)}, s32[512,8]{0,1:T(8,128)}, u32[]{:S(2)}) copy-start(s32[512,8]{0,1:T(8,128)} %param.5) | copy-start | bytes 49156
  44.1 63.6 %all-to-all-start.1 = ((bf16[8,2,10,8192]{3,1,2,0:T(2,128)(2,1)}), bf16[8,2,10,8192]{3,1,2,0:T(2,128)(2,1)}, u32[]{:S(2)}, u32[]{:S(2)}) async-start(bf16[8,2,10,8192]{3,1,2,0:T(2,128)(2,1)} %copy.96), calls=%async_computation.1 | async-start | bytes 5242880 | tf_op jit(solution)/shard_map/all_to_all | solution.py:56
  58.0 486.6 %reduce-scatter.5.cloned.1.call-start = ((), (), s32[]{:S(2)}) async-start(), calls=%async_computation.6 | async-start | bytes 266240 | tf_op jit(solution)/shard_map/reduce_scatter | solution.py:67
  60.1 934.5 %reduce-scatter.3.cloned.1.call-start = ((), (), s32[]{:S(2)}) async-start(), calls=%async_computation.5 | async-start | bytes 2662400 | tf_op jit(solution)/shard_map/reduce_scatter | solution.py:66
  995.4 6.4 copy-start.1
Sparse Core Ops, SparseCore 0:
  62.2 482.3 reduce-scatter.4
  547.5 447.0 reduce-scatter.2
